TPU v7x, 32 devices: a whole 2x2x4 slice. The times are simulated.
32 devices in a mesh: rep: 2 (over y), exp: 8 (over z, x), dec: 2 (over core).
Axes of the slice: x: 2, y: 2, z: 4, core: 2. Of those that a mesh axis runs over, the one named last changes fastest.
Arguments:
- tokens: bfloat16 [4096, 1024], P(('rep', 'exp', 'dec')), parts along dimension 0, may hold values from -6 to 6
- expert_ids: int32 [4096, 2], P(('rep', 'exp', 'dec')), parts along dimension 0, may hold values from 0 to 3, as said below
- gate_logits: float32 [4096, 2], P(('rep', 'exp', 'dec')), parts along dimension 0, may hold values from -4.25 to 4.25
- source_lengths: int32 [32], P(('rep', 'exp', 'dec')), parts along dimension 0, may hold values from 96 to 128
- page_table: int32 [32], P(('rep', 'exp', 'dec')), parts along dimension 0, may hold values from 0 to 1, as said below
- norm_gain: float32 [1024], replicated, may hold values from 0.1 to 1.9
- final_gain: float32 [1024], replicated, may hold values from 0.1 to 1.9
- w_in: bfloat16 [8, 1024, 2048], P('exp', None, 'dec'), may hold values from -0.1875 to 0.1875
- w_out: bfloat16 [8, 2048, 1024], P('exp', 'dec'), may hold values from -0.09375 to 0.09375
- w_kv: bfloat16 [1024, 2048], P(('exp', 'dec')), may hold values from -0.1875 to 0.1875
- b_kv: float32 [2048], replicated, may hold values from -3 to 3
Outputs:
- kv_pages: bfloat16 [32, 128, 2048], P(('rep', 'exp', 'dec')), parts along dimension 0
There are 2 independent parts, one for each index of `rep`. A program takes and returns all parts, laid end to end along the dimension named above; an argument that names none is the same for every part. Nothing has to cross between parts.
Inputs may be any that keep to these rules, and one draw needn't show every extreme that they name: `expert_ids`: each row names two different experts; within the rows of one device (aligned blocks of 128 rows) one expert is named exactly 96 times, all on rows before that page's length, and every other expert at most (162) // 3 times. `page_table`: pages 2 c and 2 c + 1 always go to different cores.
All inputs are finite; a program needn't handle non-finite values.
Results may differ from a plain program's by a relative error of at most 0.0053.
Values may be sent and summed in bfloat16 or wider, within the bound.
A program may use at most 64 MiB of HBM per device.

v0:
```python
import jax
import jax.numpy as jnp
from jax import lax
from jax.sharding import PartitionSpec as P

epsilon = 1e-05


def partner(value, axis, bit):
    mask = 2**bit
    pairs = [(source, source ^ mask) for source in range(lax.axis_size(axis))]
    return lax.ppermute(value, axis, pairs)


def layer_norm(values, scale_gain):
    values = values.astype(jnp.float32)
    center = values - jnp.mean(values, axis=-1, keepdims=True)
    spread = jnp.mean(center * center, axis=-1, keepdims=True)
    return center * lax.rsqrt(spread + epsilon) * scale_gain


def route_slots(expert_ids, is_valid, experts):
    pair_ids = expert_ids.reshape(-1)
    pair_live = jnp.repeat(is_valid, 2)
    onehot = (
        (pair_ids[:, None] == jnp.arange(experts, dtype=jnp.int32)[None, :]) & pair_live[:, None]
    ).astype(jnp.int32)
    before = jnp.cumsum(onehot, axis=0) - onehot
    pair_slots = jnp.sum(before * onehot, axis=1)
    return (pair_ids, pair_live, pair_slots)


def shards(
    tokens,
    expert_ids,
    gate_logits,
    source_lengths,
    page_table,
    norm_gain,
    final_gain,
    w_in,
    w_out,
    w_kv,
    b_kv,
):
    tok_rows, feature_width = tokens.shape
    experts = lax.axis_size("exp") // 2
    capacity = 2 * max(1, (3 * tok_rows + experts - 1) // (2 * experts))
    half_cap = capacity // 2
    position = jnp.arange(tok_rows, dtype=jnp.int32)
    is_valid = position < source_lengths[0]
    normed = layer_norm(tokens, norm_gain).astype(jnp.bfloat16)
    pair_ids, pair_live, pair_slots = route_slots(expert_ids, is_valid, experts)
    overflow_row = experts * capacity
    target = jnp.where(pair_live, pair_ids * capacity + pair_slots, overflow_row)
    outgoing = (
        jnp.zeros((overflow_row, feature_width), jnp.bfloat16)
        .at[target]
        .set(jnp.repeat(normed, 2, axis=0), mode="drop")
    )
    arrived = lax.all_to_all(
        outgoing.reshape(2 * experts, half_cap, feature_width),
        "exp",
        split_axis=0,
        concat_axis=0,
        tiled=True,
    )
    partner_in, partner_out = partner((w_in, w_out), "exp", 0)
    w_inner = jnp.concatenate([w_in[0], partner_in[0]], axis=1)
    w_outer = jnp.concatenate([w_out[0], partner_out[0]], axis=0)
    local_rows = arrived[None]
    block_piece = lax.all_gather(local_rows[None], "dec", axis=0, tiled=True)
    flat_rows = block_piece.reshape(-1, feature_width)
    hidden = jnp.maximum(
        jnp.dot(flat_rows, w_inner, preferred_element_type=jnp.float32), 0.0
    ).astype(jnp.bfloat16)
    partial_out = jnp.dot(hidden, w_outer, preferred_element_type=jnp.float32).reshape(
        block_piece.shape
    )
    summed = partial_out[:, 0]
    reduced = lax.psum_scatter(summed, "dec", scatter_dimension=0, tiled=True)[0].astype(
        jnp.bfloat16
    )
    returned = lax.all_to_all(reduced, "exp", split_axis=0, concat_axis=0, tiled=True).reshape(
        overflow_row, feature_width
    )
    picked = (
        returned[jnp.minimum(target, overflow_row - 1)]
        .astype(jnp.float32)
        .reshape(tok_rows, 2, feature_width)
    )
    gate_weights = jax.nn.sigmoid(gate_logits - gate_logits[:, ::-1])
    mixed_out = jnp.sum(gate_weights[:, :, None] * picked, axis=1)
    residual_sum = tokens.astype(jnp.float32) + jnp.where(is_valid[:, None], mixed_out, 0.0)
    encoded = layer_norm(residual_sum, final_gain).astype(jnp.bfloat16)
    my_core = lax.axis_index("dec")
    keep_own = page_table[0] == my_core
    page_length = source_lengths[0]
    projected = jnp.dot(
        encoded,
        lax.all_gather(w_kv, ("exp", "dec"), axis=0, tiled=True),
        preferred_element_type=jnp.float32,
    )
    keys_values = jnp.where((position < page_length)[:, None], projected + b_kv, 0.0).astype(
        jnp.bfloat16
    )
    page_result = jnp.where(keep_own, keys_values, partner(keys_values, "dec", 0))
    return page_result[None]


def solution(mesh):
    return jax.shard_map(
        shards,
        mesh=mesh,
        in_specs=(
            P(("rep", "exp", "dec"), None),
            P(("rep", "exp", "dec"), None),
            P(("rep", "exp", "dec"), None),
            P(("rep", "exp", "dec")),
            P(("rep", "exp", "dec")),
            P(),
            P(),
            P("exp", None, "dec"),
            P("exp", "dec", None),
            P(("exp", "dec"), None),
            P(),
        ),
        out_specs=P(("rep", "exp", "dec"), None, None),
        check_vma=False,
    )
```

profile of v0, /device:TPU:0, one launch (start us, length us, event | category | flops | bytes accessed | tf_op | source)
XLA Modules:
  0.0 211.7 jit_solution(16054076689131202752)
XLA Ops:
  7.4 0.9 copy.23
  9.6 0.7 broadcast_multiply_fusion
  10.6 1.2 reduce-window.6
  12.5 1.1 convert_reduce_fusion
  13.5 1.2 fusion.16
  14.7 1.2 fusion.18
  16.4 2.6 %scatter_custom_fusion = bf16[384,1024]{1,0:T(8,128)(2,1)} fusion(s32[256]{0:T(256)S(1)} %bitcast.46, bf16[256,1024]{1,0:T(8,128)(2,1)S(1)} %reshape.160, bf16[]{:T(256)} %constant.13.clone.1), kind=kCustom, calls=%fused_computation.27 | custom fusion | bytes 786434 | tf_op jit(solution)/shard_map/scatter | solution.py:59
  19.0 7.3 %all-to-all-start = ((bf16[8,48,1024]{2,1,0:T(8,128)(2,1)}), bf16[8,48,1024]{2,1,0:T(8,128)(2,1)S(1)}, u32[]{:S(2)}, u32[]{:S(2)}) async-start(bf16[8,48,1024]{2,1,0:T(8,128)(2,1)} %bitcast.6), calls=%async_computation | async-start | bytes 1572864 | tf_op jit(solution)/shard_map/all_to_all | solution.py:61
  26.3 2.0 collective-permute-start.1
  28.5 18.0 %all-to-all-done = bf16[8,48,1024]{2,1,0:T(8,128)(2,1)S(1)} async-done(((bf16[8,48,1024]{2,1,0:T(8,128)(2,1)}), bf16[8,48,1024]{2,1,0:T(8,128)(2,1)S(1)}, u32[]{:S(2)}, u32[]{:S(2)}) %all-to-all-start) | async-done | bytes 786464 | tf_op jit(solution)/shard_map/all_to_all | solution.py:61
  46.5 0.9 copy-done.1
  47.4 36.2 %collective-permute-done.1 = bf16[1,1024,1024]{2,1,0:T(8,128)(2,1)} collective-permute-done((bf16[1,1024,1024]{2,1,0:T(8,128)(2,1)S(1)}, bf16[1,1024,1024]{2,1,0:T(8,128)(2,1)}, u32[]{:S(2)}, u32[]{:S(2)}) %collective-permute-start.1) | collective-permute-done | bytes 2097184 | tf_op jit(solution)/shard_map/ppermute | solution.py:12
  83.6 43.5 %collective-permute-done = bf16[1,1024,1024]{2,1,0:T(8,128)(2,1)} collective-permute-done((bf16[1,1024,1024]{2,1,0:T(8,128)(2,1)}, bf16[1,1024,1024]{2,1,0:T(8,128)(2,1)}, u32[]{:S(2)}, u32[]{:S(2)}) %collective-permute-start) | collective-permute-done | bytes 2097184 | tf_op jit(solution)/shard_map/ppermute | solution.py:12
  127.1 11.7 %fusion.4 = f32[768,1024]{1,0:T(8,128)} fusion(bf16[1024,1024]{1,0:T(8,128)(2,1)} %bitcast.11, bf16[1024,1024]{1,0:T(8,128)(2,1)S(1)} %bitcast.47, bf16[768,1024]{1,0:T(8,128)(2,1)} %bitcast.49, bf16[1024,1024]{1,0:T(8,128)(2,1)} %bitcast.9, bf16[1024,1024]{1,0:T(8,128)(2,1)} %bitcast.48), kind=kOutput, calls=%fused_computation.7 | convolution fusion | flops 6462373888 | bytes 13107200 | tf_op jit(solution)/shard_map/dot_general | solution.py:77
  139.3 10.5 %reduce-scatter.2.cloned.1.call-done = f32[1,8,48,1024]{3,2,1,0:T(8,128)} async-done(((f32[2,8,48,1024]{3,2,1,0:T(8,128)}), f32[1,8,48,1024]{3,2,1,0:T(8,128)}) %reduce-scatter.2.cloned.1.call-update) | async-done | bytes 1572880 | tf_op jit(solution)/shard_map/reduce_scatter | solution.py:81
  149.8 2.4 %convert_bitcast_fusion = bf16[8,48,1024]{2,1,0:T(8,128)(2,1)} fusion(f32[1,8,48,1024]{3,2,1,0:T(8,128)} %reduce-scatter.2.cloned.1.call-done), kind=kLoop, calls=%fused_computation.15 | loop fusion | flops 393216 | bytes 2359296 | tf_op jit(solution)/shard_map/convert_element_type | solution.py:81
  152.2 5.8 %all-to-all-start.1 = ((bf16[8,48,1024]{2,1,0:T(8,128)(2,1)}), bf16[8,48,1024]{2,1,0:T(8,128)(2,1)S(1)}, u32[]{:S(2)}, u32[]{:S(2)}) async-start(bf16[8,48,1024]{2,1,0:T(8,128)(2,1)} %convert_bitcast_fusion), calls=%async_computation.2 | async-start | bytes 1572864 | tf_op jit(solution)/shard_map/all_to_all | solution.py:84
  158.2 30.6 %all-to-all-done.1 = bf16[8,48,1024]{2,1,0:T(8,128)(2,1)S(1)} async-done(((bf16[8,48,1024]{2,1,0:T(8,128)(2,1)}), bf16[8,48,1024]{2,1,0:T(8,128)(2,1)S(1)}, u32[]{:S(2)}, u32[]{:S(2)}) %all-to-all-start.1) | async-done | bytes 786464 | tf_op jit(solution)/shard_map/all_to_all | solution.py:84
  188.8 1.2 gather_fusion
  190.6 1.4 multiply_reduce_fusion
  192.5 5.8 %all-gather.4.cloned.1.call-done = bf16[1024,2048]{1,0:T(8,128)(2,1)} async-done(((bf16[64,2048]{1,0:T(8,128)(2,1)}), bf16[1024,2048]{1,0:T(8,128)(2,1)}) %all-gather.4.cloned.1.call-update) | async-done | bytes 4194320 | tf_op jit(solution)/shard_map/all_gather | solution.py:101
  198.3 3.1 %fusion.11 = bf16[128,2048]{1,0:T(8,128)(2,1)S(1)} fusion(bf16[1024,2048]{1,0:T(8,128)(2,1)} %all-gather.4.cloned.1.call-done, f32[2048]{0:T(1024)S(1)} %copy-done.4, pred[128]{0:T(512)(128)(4,1)S(1)} %iota_compare_fusion.1, f32[1024]{0:T(1024)S(1)} %copy-done.5, f32[128]{0:T(128)S(1)} %add_rsqrt_fusion, f32[128]{0:T(128)S(1)} %broadcast_multiply_fusion.1, ...), kind=kOutput, calls=%fused_computation.13 | convolution fusion | flops 538574848 | bytes 5518464 | tf_op jit(solution)/shard_map/dot_general | solution.py:99
  202.4 1.0 collective-permute-done.2
  203.4 0.8 select_bitcast_fusion
  (53 shorter events, 4.5 us)
Async XLA Ops:
  7.4 19.0 %copy-start.3 = (bf16[1,1024,1024]{2,1,0:T(8,128)(2,1)S(1)}, bf16[1,1024,1024]{2,1,0:T(8,128)(2,1)}, u32[]{:S(2)}) copy-start(bf16[1,1024,1024]{2,1,0:T(8,128)(2,1)} %param.19) | copy-start | bytes 6291460
  19.0 27.4 %all-to-all-start = ((bf16[8,48,1024]{2,1,0:T(8,128)(2,1)}), bf16[8,48,1024]{2,1,0:T(8,128)(2,1)S(1)}, u32[]{:S(2)}, u32[]{:S(2)}) async-start(bf16[8,48,1024]{2,1,0:T(8,128)(2,1)} %bitcast.6), calls=%async_computation | async-start | bytes 1572864 | tf_op jit(solution)/shard_map/all_to_all | solution.py:61
  26.3 100.8 %all-gather.6.cloned.1.call-start = ((), (), s32[]{:S(2)}) async-start(), calls=%async_computation.5 | async-start | bytes 2359296 | tf_op jit(solution)/shard_map/all_gather | solution.py:72
  26.3 57.2 %collective-permute-start.1 = (bf16[1,1024,1024]{2,1,0:T(8,128)(2,1)S(1)}, bf16[1,1024,1024]{2,1,0:T(8,128)(2,1)}, u32[]{:S(2)}, u32[]{:S(2)}) collective-permute-start(bf16[1,1024,1024]{2,1,0:T(8,128)(2,1)S(1)} %copy-done.3), channel_id=1, source_target_pairs={{0,2},{2,0},{4,6},{6,4},{8,10},{10,8},{12,14},{14,12},{1,3},{3,1},... | collective-permute-start | bytes 6291464 | tf_op jit(solution)/shard_map/ppermute | solution.py:12
  28.4 98.7 %collective-permute-start = (bf16[1,1024,1024]{2,1,0:T(8,128)(2,1)}, bf16[1,1024,1024]{2,1,0:T(8,128)(2,1)}, u32[]{:S(2)}, u32[]{:S(2)}) collective-permute-start(bf16[1,1024,1024]{2,1,0:T(8,128)(2,1)} %param.18), channel_id=1, source_target_pairs={{0,2},{2,0},{4,6},{6,4},{8,10},{10,8},{12,14},{14,12},{1,3},{3,1},... | collective-permute-start | bytes 6291464 | tf_op jit(solution)/shard_map/ppermute | solution.py:12
  46.5 0.9 copy-start.1
  47.4 102.4 %reduce-scatter.2.cloned.1.call-start = ((), (), s32[]{:S(2)}) async-start(), calls=%async_computation.3 | async-start | bytes 4718592 | tf_op jit(solution)/shard_map/reduce_scatter | solution.py:81
  138.7 19.2 %copy-start.2 = (f32[128,2]{0,1:T(2,128)S(1)}, f32[128,2]{0,1:T(2,128)}, u32[]{:S(2)}) copy-start(f32[128,2]{0,1:T(2,128)} %param.13) | copy-start | bytes 3076
  138.8 59.6 %all-gather.4.cloned.1.call-start = ((), (), s32[]{:S(2)}) async-start(), calls=%async_computation.4 | async-start | bytes 4456448 | tf_op jit(solution)/shard_map/all_gather | solution.py:101
  152.2 36.5 %all-to-all-start.1 = ((bf16[8,48,1024]{2,1,0:T(8,128)(2,1)}), bf16[8,48,1024]{2,1,0:T(8,128)(2,1)S(1)}, u32[]{:S(2)}, u32[]{:S(2)}) async-start(bf16[8,48,1024]{2,1,0:T(8,128)(2,1)} %convert_bitcast_fusion), calls=%async_computation.2 | async-start | bytes 1572864 | tf_op jit(solution)/shard_map/all_to_all | solution.py:84
  188.8 3.2 %copy-start = (bf16[128,1024]{1,0:T(8,128)(2,1)S(1)}, bf16[128,1024]{1,0:T(8,128)(2,1)}, u32[]{:S(2)}) copy-start(bf16[128,1024]{1,0:T(8,128)(2,1)} %param.11) | copy-start | bytes 786436
  189.9 8.4 %copy-start.4 = (f32[2048]{0:T(1024)S(1)}, f32[2048]{0:T(1024)}, u32[]{:S(2)}) copy-start(f32[2048]{0:T(1024)} %param.21) | copy-start | bytes 24580
  189.9 8.4 %copy-start.5 = (f32[1024]{0:T(1024)S(1)}, f32[1024]{0:T(1024)}, u32[]{:S(2)}) copy-start(f32[1024]{0:T(1024)} %param.17) | copy-start | bytes 12292
  201.4 2.0 collective-permute-start.2
Sparse Core Ops, SparseCore 0:
  47.5 8.8 all-gather.5
  138.9 10.8 reduce-scatter.1
Sparse Core Ops, SparseCore 1:
  141.4 56.9 all-gather.3
where the time goes:
time: 212 us
  waiting for transfers between devices  146 us (69%)
  between operations  16.3 us (8%)
  starting transfers between devices  15.6 us (7%)
  matrix products  14.7 us (7%)
  other arithmetic  10.6 us (5%)
  local copies, waits for them, and re-layouts  8.29 us (4%)
    ppermute x3, waiting for transfers between devices, partner(): return lax.ppermute(value, axis, pairs)  80.6 us
    all_to_all x1, waiting for transfers between devices, shards(): lax.all_to_all(reduced, 'exp', split_axis=0, concat_axis=0, tiled=True)  30.6 us
    all_to_all x1, waiting for transfers between devices, shards(): lax.all_to_all(outgoing.reshape(2 * experts, half_cap, feature_width), 'e...  18 us
    dot_general x1, matrix products, shards(): jnp.dot(hidden, w_outer, preferred_element_type=jnp.float32)  11.7 us
    reduce_scatter x1, waiting for transfers between devices, shards(): lax.psum_scatter(summed, 'dec', scatter_dimension=0, tiled=True)[0]  10.5 us
    all_to_all x1, starting transfers between devices, shards(): lax.all_to_all(outgoing.reshape(2 * experts, half_cap, feature_width), 'e...  7.25 us
    all_gather x1, waiting for transfers between devices, shards(): lax.all_gather(w_kv, ('exp', 'dec'), axis=0, tiled=True)  5.85 us
    all_to_all x1, starting transfers between devices, shards(): lax.all_to_all(reduced, 'exp', split_axis=0, concat_axis=0, tiled=True)  5.75 us
  transfers between devices with their start and end apart: 8, of which 7 were waited for; matrix products, arithmetic and copies ran while one was open for 3% of the time, Pallas kernels for 0%

commit v1 on v0

--- a/solution.py
+++ b/solution.py
@@ -1,9 +1,14 @@
+import functools
+
 import jax
 import jax.numpy as jnp
 from jax import lax
+from jax.experimental import pallas as pl
+from jax.experimental.pallas import tpu as pltpu
 from jax.sharding import PartitionSpec as P
 
 epsilon = 1e-05
+MESH = pl.DeviceIdType.MESH
 
 
 def partner(value, axis, bit):
@@ -108,9 +113,348 @@
     return page_result[None]
 
 
+def fused_kernel(
+    experts,
+    capacity,
+    tokens_ref,
+    ids_ref,
+    logits_ref,
+    length_ref,
+    page_ref,
+    norm_ref,
+    final_ref,
+    w_in_ref,
+    w_out_ref,
+    enc_ref,
+    live_ref,
+    wi,
+    wo,
+    pick,
+    sends,
+    held,
+    hid,
+    own_sum,
+    part_send,
+    part_recv,
+    back_send,
+    back,
+    swap_send,
+    swap_recv,
+    wl_sem,
+    ws_sem,
+    wr_sem,
+    zs_sem,
+    zr_sem,
+    xs_sem,
+    xr_sem,
+    ps_sem,
+    pr_sem,
+    bs_sem,
+    br_sem,
+    es_sem,
+    er_sem,
+):
+    rows, width = tokens_ref.shape
+    group = lax.axis_index("exp")
+    core = lax.axis_index("dec")
+    z = group // 2
+    side = group % 2
+    across = 2 * z + (1 - side)
+
+    def peer(step):
+        return lax.rem(z + step, experts)
+
+    def source(step):
+        return lax.rem(z + experts - step, experts)
+
+    barrier = pltpu.get_barrier_semaphore()
+    pl.semaphore_signal(barrier, inc=1, device_id={"dec": 1 - core}, device_id_type=MESH)
+    pl.semaphore_signal(barrier, inc=1, device_id={"exp": across}, device_id_type=MESH)
+    for step in range(1, experts):
+        pl.semaphore_signal(
+            barrier, inc=1, device_id={"exp": 2 * peer(step) + side}, device_id_type=MESH
+        )
+
+    local_weights = [
+        pltpu.make_async_copy(w_in_ref.at[0], wi.at[0], wl_sem.at[0]),
+        pltpu.make_async_copy(w_out_ref.at[0], wo.at[0], wl_sem.at[1]),
+    ]
+    for copy in local_weights:
+        copy.start()
+
+    normed = layer_norm(tokens_ref[...], norm_ref[...]).astype(jnp.bfloat16)
+    ids = ids_ref[...]
+    live = lax.broadcasted_iota(jnp.int32, (rows, 1), 0) < length_ref[...]
+    lane = lax.broadcasted_iota(jnp.int32, (rows, 128), 1)
+    named = ((ids[:, 0:1] == lane) | (ids[:, 1:2] == lane)) & live
+    earlier = lax.broadcasted_iota(jnp.int32, (rows, rows), 1) < lax.broadcasted_iota(
+        jnp.int32, (rows, rows), 0
+    )
+    count = jnp.dot(
+        earlier.astype(jnp.float32).astype(jnp.bfloat16),
+        named.astype(jnp.float32).astype(jnp.bfloat16),
+        preferred_element_type=jnp.float32,
+    ).astype(jnp.int32)
+    slots = jnp.where(named, count, -1)
+    slot_lane = lax.broadcasted_iota(jnp.int32, (rows, capacity), 1)
+    for e in range(experts):
+        chosen = (slots[:, e : e + 1] == slot_lane).astype(jnp.float32).astype(jnp.bfloat16)
+        pick[e] = chosen
+        sends[e] = lax.dot_general(
+            chosen, normed, (((0,), (0,)), ((), ())), preferred_element_type=jnp.float32
+        ).astype(jnp.bfloat16)
+
+    pl.semaphore_wait(barrier, experts + 1)
+
+    def remote(src, dst, send_sem, recv_sem, where):
+        return pltpu.make_async_remote_copy(
+            src_ref=src,
+            dst_ref=dst,
+            send_sem=send_sem,
+            recv_sem=recv_sem,
+            device_id=where,
+            device_id_type=MESH,
+        )
+
+    dispatch = []
+    for step in range(1, experts):
+        to = peer(step)
+        copy = remote(
+            sends.at[to],
+            held.at[0, z],
+            zs_sem.at[step],
+            zr_sem.at[step],
+            {"exp": 2 * to + side},
+        )
+        copy.start()
+        dispatch.append(copy)
+    held[0, z] = sends[z]
+
+    swap_weights = [
+        remote(w_in_ref.at[0], wi.at[1], ws_sem.at[0], wr_sem.at[0], {"dec": 1 - core}),
+        remote(w_out_ref.at[0], wo.at[1], ws_sem.at[1], wr_sem.at[1], {"dec": 1 - core}),
+    ]
+
+    def forward(step):
+        at = source(step)
+        copy = remote(
+            held.at[0, at], held.at[1, at], xs_sem.at[step], xr_sem.at[step], {"exp": across}
+        )
+        copy.start()
+        return copy
+
+    def part_copy(step):
+        return remote(
+            part_send.at[step],
+            part_recv.at[step],
+            ps_sem.at[step],
+            pr_sem.at[step],
+            {"exp": across},
+        )
+
+    def back_copy(step):
+        return remote(
+            back_send.at[step],
+            back.at[z],
+            bs_sem.at[step],
+            br_sem.at[step],
+            {"exp": 2 * source(step) + side},
+        )
+
+    unit = wi.shape[2]
+    tile = 512
+
+    def ffn(column, at, store):
+        def inner(i, carry):
+            half = i // (unit // tile)
+            offset = pl.multiple_of(i % (unit // tile) * tile, tile)
+            block = jnp.dot(
+                held[column, at],
+                wi[half, :, pl.ds(offset, tile)],
+                preferred_element_type=jnp.float32,
+            )
+            hid[half, :, pl.ds(offset, tile)] = jnp.maximum(block, 0.0).astype(jnp.bfloat16)
+            return carry
+
+        lax.fori_loop(0, 2 * (unit // tile), inner, 0)
+
+        def outer(i, carry):
+            cols = pl.ds(pl.multiple_of(i * tile, tile), tile)
+            total = jnp.dot(hid[0], wo[0, :, cols], preferred_element_type=jnp.float32)
+            total += jnp.dot(hid[1], wo[1, :, cols], preferred_element_type=jnp.float32)
+            store(cols, total)
+            return carry
+
+        lax.fori_loop(0, width // tile, outer, 0)
+
+    def ffn_own(step):
+        def store(cols, total):
+            own_sum[step, :, cols] = total
+
+        ffn(0, source(step), store)
+
+    def ffn_other(step):
+        def store(cols, total):
+            part_send[step, :, cols] = total.astype(jnp.bfloat16)
+
+        ffn(1, source(step), store)
+        part_copy(step).start()
+
+    def finish(step):
+        part_copy(step).wait_recv()
+        total = (own_sum[step] + part_recv[step].astype(jnp.float32)).astype(jnp.bfloat16)
+        if step == 0:
+            back[z] = total
+        else:
+            back_send[step] = total
+            back_copy(step).start()
+
+    forwards = [forward(0)]
+    for copy in swap_weights:
+        copy.start()
+    for copy in local_weights:
+        copy.wait()
+    for copy in swap_weights:
+        copy.wait_recv()
+    ffn_own(0)
+    for step in range(1, experts):
+        dispatch[step - 1].wait_recv()
+        forwards.append(forward(step))
+        forwards[step - 1].wait_recv()
+        ffn_other(step - 1)
+        ffn_own(step)
+        if step >= 2:
+            finish(step - 2)
+    forwards[experts - 1].wait_recv()
+    ffn_other(experts - 1)
+    finish(experts - 2)
+    finish(experts - 1)
+
+    logits = logits_ref[...]
+    gates = jax.nn.sigmoid(logits[:, 0:1] - logits[:, 1:2])
+    gates_other = jax.nn.sigmoid(logits[:, 1:2] - logits[:, 0:1])
+    residual = tokens_ref[...].astype(jnp.float32)
+    for step in range(experts):
+        if step > 0:
+            back_copy(step).wait_recv()
+        e = peer(step)
+        gate = jnp.where(ids[:, 0:1] == e, gates, gates_other)
+        residual += gate * jnp.dot(pick[e], back[e], preferred_element_type=jnp.float32)
+    encoded = layer_norm(residual, final_ref[...]).astype(jnp.bfloat16)
+    mask = jnp.broadcast_to(live, (rows, 128)).astype(jnp.float32).astype(jnp.bfloat16)
+    swap_send[:, :width] = encoded
+    swap_send[:, width:] = mask
+    exchange = remote(swap_send, swap_recv, es_sem, er_sem, {"dec": 1 - core})
+    exchange.start()
+
+    for copy in swap_weights + dispatch + forwards:
+        copy.wait_send()
+    for step in range(experts):
+        part_copy(step).wait_send()
+        if step > 0:
+            back_copy(step).wait_send()
+    exchange.wait()
+    keep = page_ref[...] == core
+    mine = swap_send[...].astype(jnp.float32)
+    other = swap_recv[...].astype(jnp.float32)
+    final = jnp.where(keep, mine, other).astype(jnp.bfloat16)
+    enc_ref[...] = final[:, :width]
+    live_ref[...] = final[:, width:]
+
+
+def fused(
+    capacity,
+    tokens,
+    expert_ids,
+    gate_logits,
+    source_lengths,
+    page_table,
+    norm_gain,
+    final_gain,
+    w_in,
+    w_out,
+):
+    rows, width = tokens.shape
+    unit = w_in.shape[2]
+    experts = lax.axis_size("exp") // 2
+    bf16 = jnp.bfloat16
+    block = (experts, capacity, width)
+    dma = pltpu.SemaphoreType.DMA
+    vmem = pl.BlockSpec(memory_space=pltpu.VMEM)
+    anywhere = pl.BlockSpec(memory_space=pl.ANY)
+    return pl.pallas_call(
+        functools.partial(fused_kernel, experts, capacity),
+        out_shape=(
+            jax.ShapeDtypeStruct((rows, width), bf16),
+            jax.ShapeDtypeStruct((rows, 128), bf16),
+        ),
+        in_specs=[vmem] * 7 + [anywhere] * 2,
+        out_specs=(vmem, vmem),
+        scratch_shapes=[
+            pltpu.VMEM((2,) + w_in.shape[1:], bf16),
+            pltpu.VMEM((2,) + w_out.shape[1:], bf16),
+            pltpu.VMEM((experts, rows, capacity), bf16),
+            pltpu.VMEM(block, bf16),
+            pltpu.VMEM((2,) + block, bf16),
+            pltpu.VMEM((2, capacity, unit), bf16),
+            pltpu.VMEM(block, jnp.float32),
+            pltpu.VMEM(block, bf16),
+            pltpu.VMEM(block, bf16),
+            pltpu.VMEM(block, bf16),
+            pltpu.VMEM(block, bf16),
+            pltpu.VMEM((rows, width + 128), bf16),
+            pltpu.VMEM((rows, width + 128), bf16),
+            dma((2,)),
+            dma((2,)),
+            dma((2,)),
+        ]
+        + [dma((experts,)) for _ in range(8)]
+        + [dma, dma],
+        compiler_params=pltpu.CompilerParams(
+            collective_id=0, has_side_effects=True, vmem_limit_bytes=40 * 1024 * 1024
+        ),
+        cost_estimate=pl.CostEstimate(
+            flops=8 * experts * capacity * width * unit * 2,
+            bytes_accessed=64 * 1024 * 1024,
+            transcendentals=0,
+        ),
+        name="expert_layer",
+    )(
+        tokens,
+        expert_ids,
+        gate_logits,
+        source_lengths.reshape(1, 1),
+        page_table.reshape(1, 1),
+        norm_gain.reshape(1, width),
+        final_gain.reshape(1, width),
+        w_in,
+        w_out,
+    )
+
+
+def kernel_shards(capacity, *args):
+    tokens, ids, logits, lengths, pages, norm_gain, final_gain, w_in, w_out, w_kv, b_kv = args
+    w_full = lax.all_gather(w_kv, ("exp", "dec"), axis=0, tiled=True)
+    encoded, live = fused(
+        capacity, tokens, ids, logits, lengths, pages, norm_gain, final_gain, w_in, w_out
+    )
+    projected = jnp.dot(encoded, w_full, preferred_element_type=jnp.float32)
+    keys_values = jnp.where(live[:, 0:1] > 0, projected + b_kv, 0.0).astype(jnp.bfloat16)
+    return keys_values[None]
+
+
+def any_shards(*args):
+    tok_rows = args[0].shape[0]
+    experts = lax.axis_size("exp") // 2
+    capacity = 2 * max(1, (3 * tok_rows + experts - 1) // (2 * experts))
+    if capacity % 16 == 0 and experts <= 8 and lax.axis_size("dec") == 2:
+        return kernel_shards(capacity, *args)
+    return shards(*args)
+
+
 def solution(mesh):
     return jax.shard_map(
-        shards,
+        any_shards,
         mesh=mesh,
         in_specs=(
             P(("rep", "exp", "dec"), None),

time: 212 us -> 106 us (0.50)
  waiting for transfers between devices: 146 us -> 0.73 us
  Pallas kernels: 0 us -> 78.8 us
  starting transfers between devices: 15.6 us -> 0.01 us
  matrix products: 14.7 us -> 3.71 us
  other arithmetic: 10.6 us -> 0.11 us
    ppermute x3 -> x0, waiting for transfers between devices: 80.6 us -> none  [partner(): return lax.ppermute(value, axis, pairs)]
    pallas_call x0 -> x1, Pallas kernels: none -> 78.8 us  [fused(): pl.pallas_call(functools.partial(fused_kernel, experts, capacity), out_sh...]
    all_to_all x2 -> x0, waiting for transfers between devices: 48.6 us -> none  [the longest x1 30.6 us: shards(): lax.all_to_all(reduced, 'exp', split_axis=0, concat_axis=0, tiled=True)]
    all_to_all x2 -> x0, starting transfers between devices: 13 us -> none  [the longest x1 7.25 us: shards(): lax.all_to_all(outgoing.reshape(2 * experts, half_cap, feature_width), 'e...]
    dot_general x2 -> x1, matrix products: 14.7 us -> 3.71 us  [kernel_shards(): projected = jnp.dot(encoded, w_full, preferred_element_type=jnp.float32)]
    reduce_scatter x1 -> x0, waiting for transfers between devices: 10.5 us -> none  [shards(): lax.psum_scatter(summed, 'dec', scatter_dimension=0, tiled=True)[0]]
    all_gather x2 -> x1, waiting for transfers between devices: 5.85 us -> 0.02 us  [kernel_shards(): w_full = lax.all_gather(w_kv, ('exp', 'dec'), axis=0, tiled=True)]
    unnamed x13 -> x14, local copies, waits for them, and re-layouts: 1.84 us -> 7.07 us
  transfers between devices with their start and end apart: 8 -> 1, of which waited for: 7 -> 0; matrix products, arithmetic and copies ran while one was open for 3% -> 2% of each run, Pallas kernels for 0% -> 75%
where the time goes in v1:
time: 106 us; the launch traced here: 105 us
  Pallas kernels  78.8 us (74%)
  between operations  14.7 us (14%)
  local copies, waits for them, and re-layouts  7.07 us (7%)
  matrix products  3.71 us (4%)
    pallas_call x1, Pallas kernels, fused(): pl.pallas_call(functools.partial(fused_kernel, experts, capacity), out_sh...  78.8 us
    unnamed x14, local copies, waits for them, and re-layouts  7.07 us
    dot_general x1, matrix products, kernel_shards(): projected = jnp.dot(encoded, w_full, preferred_element_type=jnp.float32)  3.71 us
  transfers between devices with their start and end apart: 1, of which 0 were waited for; matrix products, arithmetic and copies ran while one was open for 2% of the time, Pallas kernels for 75%

profile of v1, /device:TPU:0, one launch (start us, length us, event | category | flops | bytes accessed | tf_op | source)
XLA Modules:
  0.0 105.2 jit_solution(4105514972974560213)
XLA Ops:
  6.5 0.0 all-gather.2.cloned.1.call-start
  6.5 0.7 all-gather.2.cloned.1.call-update
  8.5 0.8 copy.14.ids_ref
  9.3 0.8 copy.15.logits_ref
  10.1 0.0 copy-start
  10.1 1.6 %copy-done = bf16[1,1024,1024]{2,1,0:T(8,128)(2,1)S(1)} copy-done((bf16[1,1024,1024]{2,1,0:T(8,128)(2,1)S(1)}, bf16[1,1024,1024]{2,1,0:T(8,128)(2,1)}, u32[]{:S(2)}) %copy-start) | copy-done | bytes 2097176
  11.7 0.0 copy-start.1
  11.7 1.6 %copy-done.1 = bf16[1,1024,1024]{2,1,0:T(8,128)(2,1)S(1)} copy-done((bf16[1,1024,1024]{2,1,0:T(8,128)(2,1)S(1)}, bf16[1,1024,1024]{2,1,0:T(8,128)(2,1)}, u32[]{:S(2)}) %copy-start.1) | copy-done | bytes 2097176
  13.3 0.0 copy-start.2
  13.3 0.9 copy-done.2
  14.3 0.0 copy-start.3
  14.3 0.7 copy-done.3
  14.9 0.0 copy-start.4
  14.9 0.7 copy-done.4
  15.6 0.0 copy-start.5
  15.6 78.8 %expert_layer.1 = (bf16[128,1024]{1,0:T(8,128)(2,1)S(1)}, bf16[128,128]{1,0:T(8,128)(2,1)S(1)}) custom-call(bf16[128,1024]{1,0:T(8,128)(2,1)S(1)} %copy-done.2, s32[128,2]{1,0:T(8,128)S(1)} %copy.14.ids_ref, f32[128,2]{1,0:T(8,128)S(1)} %copy.15.logits_ref, s32[1,1]{1,0:T(1,128)} %bitcast.8.length_ref, s32[1,1]{1,0:T(1,128)} %bitcast.9.page_ref, ...), custom_call_target="tpu_custom_call" | custom-call | flops 6442450944 | bytes 67108864 | tf_op jit(solution)/shard_map/expert_layer/pallas_call | solution.py:385
  94.5 0.1 compare_reduce_fusion
  94.6 0.0 all-gather.2.cloned.1.call-done
  94.6 0.0 copy-done.5
  94.6 3.7 %fusion.2 = bf16[1,128,2048]{2,1,0:T(8,128)(2,1)} fusion(bf16[128,1024]{1,0:T(8,128)(2,1)S(1)} %get-tuple-element.8, bf16[1024,2048]{1,0:T(8,128)(2,1)} %all-gather.2.cloned.1.call-done, f32[2048]{0:T(1024)S(1)} %copy-done.5, pred[128]{0:T(512)(128)(4,1)S(1)} %compare_reduce_fusion), kind=kOutput, calls=%fused_computation.3 | convolution fusion | flops 537657344 | bytes 4989056 | tf_op jit(solution)/shard_map/dot_general | solution.py:441
Async XLA Ops:
  6.5 88.0 %all-gather.2.cloned.1.call-start = ((), (), s32[]{:S(2)}) async-start(), calls=%async_computation | async-start | bytes 4456448 | tf_op jit(solution)/shard_map/all_gather | solution.py:437
  10.1 1.6 %copy-start = (bf16[1,1024,1024]{2,1,0:T(8,128)(2,1)S(1)}, bf16[1,1024,1024]{2,1,0:T(8,128)(2,1)}, u32[]{:S(2)}) copy-start(bf16[1,1024,1024]{2,1,0:T(8,128)(2,1)} %w_in_ref.1) | copy-start | bytes 6291460
  11.7 1.6 %copy-start.1 = (bf16[1,1024,1024]{2,1,0:T(8,128)(2,1)S(1)}, bf16[1,1024,1024]{2,1,0:T(8,128)(2,1)}, u32[]{:S(2)}) copy-start(bf16[1,1024,1024]{2,1,0:T(8,128)(2,1)} %w_out_ref.1) | copy-start | bytes 6291460
  13.3 0.9 copy-start.2
  14.3 0.7 copy-start.3
  14.9 0.7 copy-start.4
  15.6 79.0 %copy-start.5 = (f32[2048]{0:T(1024)S(1)}, f32[2048]{0:T(1024)}, u32[]{:S(2)}) copy-start(f32[2048]{0:T(1024)} %param.21) | copy-start | bytes 24580
Sparse Core Ops, SparseCore 0:
  9.5 76.3 all-gather.1

commit v2 on v1

--- a/solution.py
+++ b/solution.py
@@ -125,8 +125,17 @@
     final_ref,
     w_in_ref,
     w_out_ref,
-    enc_ref,
-    live_ref,
+    w_kv_ref,
+    b_kv_ref,
+    kv_ref,
+    tok,
+    ids_t,
+    logits_t,
+    norm,
+    final,
+    bias,
+    kv,
+    wk,
     wi,
     wo,
     pick,
@@ -153,23 +162,56 @@
     br_sem,
     es_sem,
     er_sem,
+    in_sem,
+    kl_sem,
+    zks_sem,
+    zkr_sem,
+    zls_sem,
+    zlr_sem,
+    xks_sem,
+    xkr_sem,
+    yks_sem,
+    ykr_sem,
+    dks_sem,
+    dkr_sem,
+    kv_sem,
 ):
     rows, width = tokens_ref.shape
     group = lax.axis_index("exp")
+    part = lax.axis_index("rep")
     core = lax.axis_index("dec")
     z = group // 2
     side = group % 2
     across = 2 * z + (1 - side)
 
     def peer(step):
-        return lax.rem(z + step, experts)
-
-    def source(step):
-        return lax.rem(z + experts - step, experts)
+        other, bit = 0, 1
+        while bit < experts:
+            mine, flip = (z // bit) % 2, (step // bit) % 2
+            other = other + bit * (mine + flip - 2 * mine * flip)
+            bit *= 2
+        return other
+
+    inputs = [
+        pltpu.make_async_copy(src, dst, in_sem.at[i])
+        for i, (src, dst) in enumerate(
+            (
+                (tokens_ref, tok),
+                (ids_ref, ids_t),
+                (logits_ref, logits_t),
+                (norm_ref, norm),
+                (final_ref, final),
+                (b_kv_ref, bias),
+            )
+        )
+    ]
+    for copy in inputs:
+        copy.start()
 
     barrier = pltpu.get_barrier_semaphore()
     pl.semaphore_signal(barrier, inc=1, device_id={"dec": 1 - core}, device_id_type=MESH)
     pl.semaphore_signal(barrier, inc=1, device_id={"exp": across}, device_id_type=MESH)
+    pl.semaphore_signal(barrier, inc=1, device_id={"rep": 1 - part}, device_id_type=MESH)
     for step in range(1, experts):
         pl.semaphore_signal(
             barrier, inc=1, device_id={"exp": 2 * peer(step) + side}, device_id_type=MESH
@@ -182,14 +224,21 @@
     for copy in local_weights:
         copy.start()
 
-    normed = layer_norm(tokens_ref[...], norm_ref[...]).astype(jnp.bfloat16)
-    ids = ids_ref[...]
-    live = lax.broadcasted_iota(jnp.int32, (rows, 1), 0) < length_ref[...]
+    for copy in inputs:
+        copy.wait()
+    normed = layer_norm(tok[...], norm[...]).astype(jnp.bfloat16)
+    row = lax.broadcasted_iota(jnp.int32, (rows, rows), 0)
+    column = lax.broadcasted_iota(jnp.int32, (rows, rows), 1)
+
+    def upright(line):
+        return jnp.sum(jnp.where(row == column, line, 0.0), axis=1, keepdims=True)
+
+    ids_f = ids_t[...].astype(jnp.float32)
+    first, second = (upright(ids_f[k : k + 1]).astype(jnp.int32) for k in range(2))
+    live = lax.broadcasted_iota(jnp.int32, (rows, 1), 0) < length_ref[0]
     lane = lax.broadcasted_iota(jnp.int32, (rows, 128), 1)
-    named = ((ids[:, 0:1] == lane) | (ids[:, 1:2] == lane)) & live
-    earlier = lax.broadcasted_iota(jnp.int32, (rows, rows), 1) < lax.broadcasted_iota(
-        jnp.int32, (rows, rows), 0
-    )
+    named = ((first == lane) | (second == lane)) & live
+    earlier = column < row
     count = jnp.dot(
         earlier.astype(jnp.float32).astype(jnp.bfloat16),
         named.astype(jnp.float32).astype(jnp.bfloat16),
@@ -204,7 +253,7 @@
             chosen, normed, (((0,), (0,)), ((), ())), preferred_element_type=jnp.float32
         ).astype(jnp.bfloat16)
 
-    pl.semaphore_wait(barrier, experts + 1)
+    pl.semaphore_wait(barrier, experts + 2)
 
     def remote(src, dst, send_sem, recv_sem, where):
         return pltpu.make_async_remote_copy(
@@ -216,19 +265,85 @@
             device_id_type=MESH,
         )
 
-    dispatch = []
-    for step in range(1, experts):
+    def dispatch(step):
         to = peer(step)
-        copy = remote(
+        return remote(
             sends.at[to],
             held.at[0, z],
             zs_sem.at[step],
             zr_sem.at[step],
             {"exp": 2 * to + side},
         )
-        copy.start()
-        dispatch.append(copy)
-    held[0, z] = sends[z]
+
+    block_rows = w_kv_ref.shape[0]
+    half_rows = block_rows // 2
+
+    def block(at, column_side, half):
+        start = ((2 * at + column_side) * 2 + core) * block_rows + half * half_rows
+        return wk.at[pl.ds(pl.multiple_of(start, half_rows), half_rows)]
+
+    own_start = pl.multiple_of((2 * group + core) * block_rows, block_rows)
+    own_block = wk.at[pl.ds(own_start, block_rows)]
+    own_half = w_kv_ref.at[pl.ds(pl.multiple_of(part * half_rows, half_rows), half_rows)]
+    load_block = pltpu.make_async_copy(w_kv_ref, own_block, kl_sem)
+
+    def kv_z(step):
+        where = {"exp": 2 * peer(step) + side}
+        return remote(
+            own_half, block(z, side, part), zks_sem.at[step], zkr_sem.at[step], where
+        )
+
+    def kv_z_other(step):
+        where = {"exp": 2 * peer(step) + side}
+        piece = block(z, 1 - side, part)
+        return remote(piece, piece, zls_sem.at[step], zlr_sem.at[step], where)
+
+    def kv_x(step):
+        piece = block(peer(step), side, part)
+        source = own_half if step == 0 else piece
+        return remote(source, piece, xks_sem.at[step], xkr_sem.at[step], {"exp": across})
+
+    def kv_y(other, step):
+        piece = block(peer(step), 1 - side if other else side, part)
+        index = other * experts + step
+        return remote(
+            piece, piece, yks_sem.at[index], ykr_sem.at[index], {"rep": 1 - part}
+        )
+
+    def kv_core(late, other, step):
+        index = (late * 2 + other) * experts + step
+        where = {"dec": 1 - core}
+        if other == 0 and step == 0:
+            return remote(w_kv_ref, own_block, dks_sem.at[index], dkr_sem.at[index], where)
+        half = 1 - part if late else part
+        piece = block(peer(step), 1 - side if other else side, half)
+        return remote(piece, piece, dks_sem.at[index], dkr_sem.at[index], where)
+
+    pieces = [(0, step) for step in range(1, experts)] + [(1, step) for step in range(experts)]
+    paired = [step for step in range(experts) if step % 2 == 0]
+    unpaired = [step for step in range(experts) if step % 2 == 1]
+
+    def got_own(step):
+        kv_z(step).wait_recv()
+        if step in paired:
+            kv_x(step).start()
+        kv_y(0, step).start()
+        kv_core(0, 0, step).start()
+
+    def got_other(step):
+        if step in paired:
+            kv_x(step).wait_recv()
+        else:
+            kv_z_other(step).wait_recv()
+        if step == 0:
+            for towards in unpaired:
+                kv_z_other(towards).start()
+        kv_y(1, step).start()
+        kv_core(0, 1, step).start()
+
+    def got_part(other, step):
+        kv_y(other, step).wait_recv()
+        kv_core(1, other, step).start()
 
     swap_weights = [
         remote(w_in_ref.at[0], wi.at[1], ws_sem.at[0], wr_sem.at[0], {"dec": 1 - core}),
@@ -236,12 +351,10 @@
     ]
 
     def forward(step):
-        at = source(step)
-        copy = remote(
+        at = peer(step)
+        return remote(
             held.at[0, at], held.at[1, at], xs_sem.at[step], xr_sem.at[step], {"exp": across}
         )
-        copy.start()
-        return copy
 
     def part_copy(step):
         return remote(
@@ -258,7 +371,7 @@
             back.at[z],
             bs_sem.at[step],
             br_sem.at[step],
-            {"exp": 2 * source(step) + side},
+            {"exp": 2 * peer(step) + side},
         )
 
     unit = wi.shape[2]
@@ -291,13 +404,13 @@
         def store(cols, total):
             own_sum[step, :, cols] = total
 
-        ffn(0, source(step), store)
+        ffn(0, peer(step), store)
 
     def ffn_other(step):
         def store(cols, total):
             part_send[step, :, cols] = total.astype(jnp.bfloat16)
 
-        ffn(1, source(step), store)
+        ffn(1, peer(step), store)
         part_copy(step).start()
 
     def finish(step):
@@ -309,60 +422,122 @@
             back_send[step] = total
             back_copy(step).start()
 
-    forwards = [forward(0)]
+    order = unpaired + paired[1:]
+    for step in unpaired:
+        dispatch(step).start()
+    for step in unpaired:
+        kv_z(step).start()
+    for step in paired[1:]:
+        dispatch(step).start()
+    for step in paired[1:]:
+        kv_z(step).start()
+    held[0, z] = sends[z]
+    forward(0).start()
+    kv_x(0).start()
     for copy in swap_weights:
         copy.start()
+    load_block.start()
+    kv_core(0, 0, 0).start()
     for copy in local_weights:
         copy.wait()
     for copy in swap_weights:
         copy.wait_recv()
     ffn_own(0)
+    for step in unpaired:
+        dispatch(step).wait_recv()
+        forward(step).start()
+    got_other(0)
+    for step in unpaired:
+        got_own(step)
+    previous = [0] + order[:-1]
+    for at, step in enumerate(order):
+        forward(previous[at]).wait_recv()
+        ffn_other(previous[at])
+        if at > 0:
+            finish(previous[at - 1])
+        if step in paired:
+            dispatch(step).wait_recv()
+            forward(step).start()
+            got_own(step)
+        ffn_own(step)
+    for step in unpaired:
+        got_other(step)
+    forward(order[-1]).wait_recv()
+    ffn_other(order[-1])
+    for step in paired[1:]:
+        got_other(step)
+    got_part(1, 0)
+    finish(previous[-1])
+    for step in unpaired:
+        got_part(0, step)
+    finish(order[-1])
+    for step in paired[1:]:
+        got_part(0, step)
     for step in range(1, experts):
-        dispatch[step - 1].wait_recv()
-        forwards.append(forward(step))
-        forwards[step - 1].wait_recv()
-        ffn_other(step - 1)
-        ffn_own(step)
-        if step >= 2:
-            finish(step - 2)
-    forwards[experts - 1].wait_recv()
-    ffn_other(experts - 1)
-    finish(experts - 2)
-    finish(experts - 1)
-
-    logits = logits_ref[...]
-    gates = jax.nn.sigmoid(logits[:, 0:1] - logits[:, 1:2])
-    gates_other = jax.nn.sigmoid(logits[:, 1:2] - logits[:, 0:1])
-    residual = tokens_ref[...].astype(jnp.float32)
-    for step in range(experts):
+        got_part(1, step)
+
+    logits = logits_t[...]
+    gates = upright(jax.nn.sigmoid(logits[0:1] - logits[1:2]))
+    gates_other = upright(jax.nn.sigmoid(logits[1:2] - logits[0:1]))
+    residual = tok[...].astype(jnp.float32)
+    for step in [0] + order:
         if step > 0:
             back_copy(step).wait_recv()
         e = peer(step)
-        gate = jnp.where(ids[:, 0:1] == e, gates, gates_other)
+        gate = jnp.where(first == e, gates, gates_other)
         residual += gate * jnp.dot(pick[e], back[e], preferred_element_type=jnp.float32)
-    encoded = layer_norm(residual, final_ref[...]).astype(jnp.bfloat16)
+    encoded = layer_norm(residual, final[...]).astype(jnp.bfloat16)
     mask = jnp.broadcast_to(live, (rows, 128)).astype(jnp.float32).astype(jnp.bfloat16)
     swap_send[:, :width] = encoded
     swap_send[:, width:] = mask
     exchange = remote(swap_send, swap_recv, es_sem, er_sem, {"dec": 1 - core})
     exchange.start()
 
-    for copy in swap_weights + dispatch + forwards:
+    load_block.wait()
+    kv_core(0, 0, 0).wait_recv()
+    for other, step in pieces:
+        kv_core(0, other, step).wait_recv()
+        kv_core(1, other, step).wait_recv()
+    exchange.wait_recv()
+    keep = page_ref[0] == core
+    kept = jnp.where(
+        keep, swap_send[...].astype(jnp.float32), swap_recv[...].astype(jnp.float32)
+    )
+    rows_kept = kept[:, :width].astype(jnp.bfloat16)
+    alive = kept[:, width : width + 1] > 0
+    writes = []
+    for i in range(kv.shape[1] // tile):
+        cols = pl.ds(i * tile, tile)
+        total = jnp.dot(rows_kept, wk[:, cols], preferred_element_type=jnp.float32)
+        kv[:, cols] = jnp.where(alive, total + bias[:, cols], 0.0).astype(jnp.bfloat16)
+        write = pltpu.make_async_copy(kv.at[:, cols], kv_ref.at[0, :, cols], kv_sem.at[i])
+        write.start()
+        writes.append(write)
+
+    for copy in swap_weights:
         copy.wait_send()
     for step in range(experts):
+        forward(step).wait_send()
         part_copy(step).wait_send()
         if step > 0:
+            dispatch(step).wait_send()
             back_copy(step).wait_send()
-    exchange.wait()
-    keep = page_ref[...] == core
-    mine = swap_send[...].astype(jnp.float32)
-    other = swap_recv[...].astype(jnp.float32)
-    final = jnp.where(keep, mine, other).astype(jnp.bfloat16)
-    enc_ref[...] = final[:, :width]
-    live_ref[...] = final[:, width:]
-
-
-def fused(
+            kv_z(step).wait_send()
+        if step in paired:
+            kv_x(step).wait_send()
+        else:
+            kv_z_other(step).wait_send()
+    kv_core(0, 0, 0).wait_send()
+    for other, step in pieces:
+        kv_y(other, step).wait_send()
+        kv_core(0, other, step).wait_send()
+        kv_core(1, other, step).wait_send()
+    exchange.wait_send()
+    for write in writes:
+        write.wait()
+
+
+def kernel_shards(
     capacity,
     tokens,
     expert_ids,
@@ -373,24 +548,32 @@
     final_gain,
     w_in,
     w_out,
+    w_kv,
+    b_kv,
 ):
     rows, width = tokens.shape
     unit = w_in.shape[2]
+    columns = w_kv.shape[1]
     experts = lax.axis_size("exp") // 2
     bf16 = jnp.bfloat16
     block = (experts, capacity, width)
     dma = pltpu.SemaphoreType.DMA
-    vmem = pl.BlockSpec(memory_space=pltpu.VMEM)
+    scalar = pl.BlockSpec(memory_space=pltpu.SMEM)
     anywhere = pl.BlockSpec(memory_space=pl.ANY)
     return pl.pallas_call(
         functools.partial(fused_kernel, experts, capacity),
-        out_shape=(
-            jax.ShapeDtypeStruct((rows, width), bf16),
-            jax.ShapeDtypeStruct((rows, 128), bf16),
-        ),
-        in_specs=[vmem] * 7 + [anywhere] * 2,
-        out_specs=(vmem, vmem),
+        out_shape=jax.ShapeDtypeStruct((1, rows, columns), bf16),
+        in_specs=[anywhere] * 3 + [scalar] * 2 + [anywhere] * 6,
+        out_specs=anywhere,
         scratch_shapes=[
+            pltpu.VMEM((rows, width), bf16),
+            pltpu.VMEM((2, rows), jnp.int32),
+            pltpu.VMEM((2, rows), jnp.float32),
+            pltpu.VMEM((1, width), jnp.float32),
+            pltpu.VMEM((1, width), jnp.float32),
+            pltpu.VMEM((1, columns), jnp.float32),
+            pltpu.VMEM((rows, columns), bf16),
+            pltpu.VMEM((width, columns), bf16),
             pltpu.VMEM((2,) + w_in.shape[1:], bf16),
             pltpu.VMEM((2,) + w_out.shape[1:], bf16),
             pltpu.VMEM((experts, rows, capacity), bf16),
@@ -409,45 +592,41 @@
             dma((2,)),
         ]
         + [dma((experts,)) for _ in range(8)]
-        + [dma, dma],
+        + [dma, dma, dma((6,)), dma]
+        + [dma((experts,)) for _ in range(6)]
+        + [dma((2 * experts,)) for _ in range(2)]
+        + [dma((4 * experts,)) for _ in range(2)]
+        + [dma((columns // 512,))],
         compiler_params=pltpu.CompilerParams(
-            collective_id=0, has_side_effects=True, vmem_limit_bytes=40 * 1024 * 1024
+            collective_id=0, has_side_effects=True, vmem_limit_bytes=60 * 1024 * 1024
         ),
         cost_estimate=pl.CostEstimate(
             flops=8 * experts * capacity * width * unit * 2,
-            bytes_accessed=64 * 1024 * 1024,
+            bytes_accessed=16 * 1024 * 1024,
             transcendentals=0,
         ),
         name="expert_layer",
     )(
         tokens,
-        expert_ids,
-        gate_logits,
-        source_lengths.reshape(1, 1),
-        page_table.reshape(1, 1),
+        expert_ids.T,
+        gate_logits.T,
+        source_lengths,
+        page_table,
         norm_gain.reshape(1, width),
         final_gain.reshape(1, width),
         w_in,
         w_out,
-    )
-
-
-def kernel_shards(capacity, *args):
-    tokens, ids, logits, lengths, pages, norm_gain, final_gain, w_in, w_out, w_kv, b_kv = args
-    w_full = lax.all_gather(w_kv, ("exp", "dec"), axis=0, tiled=True)
-    encoded, live = fused(
-        capacity, tokens, ids, logits, lengths, pages, norm_gain, final_gain, w_in, w_out
-    )
-    projected = jnp.dot(encoded, w_full, preferred_element_type=jnp.float32)
-    keys_values = jnp.where(live[:, 0:1] > 0, projected + b_kv, 0.0).astype(jnp.bfloat16)
-    return keys_values[None]
+        w_kv,
+        b_kv.reshape(1, columns),
+    )
 
 
 def any_shards(*args):
     tok_rows = args[0].shape[0]
     experts = lax.axis_size("exp") // 2
     capacity = 2 * max(1, (3 * tok_rows + experts - 1) // (2 * experts))
-    if capacity % 16 == 0 and experts <= 8 and lax.axis_size("dec") == 2:
+    whole_tiles = capacity % 16 == 0 and args[9].shape[0] % 32 == 0
+    if whole_tiles and experts == 4 and lax.axis_size("dec") == lax.axis_size("rep") == 2:
         return kernel_shards(capacity, *args)
     return shards(*args)
 

time: 106 us -> 70.5 us (0.67)
  between operations: 14.7 us -> 1.3 us
  Pallas kernels: 78.8 us -> 66 us
  local copies, waits for them, and re-layouts: 7.07 us -> 1.88 us
  matrix products: 3.71 us -> 0 us
    pallas_call x1, Pallas kernels: 78.8 us -> 66 us  [kernel_shards(): pl.pallas_call(functools.partial(fused_kernel, experts, capacity), out_sh...]
    unnamed x14 -> x1, local copies, waits for them, and re-layouts: 7.07 us -> 1.88 us
    dot_general x1 -> x0, matrix products: 3.71 us -> none  [kernel_shards(): projected = jnp.dot(encoded, w_full, preferred_element_type=jnp.float32)]
  transfers between devices with their start and end apart: 1 -> 0, of which waited for: 0 -> 0; matrix products, arithmetic and copies ran while one was open for 2% -> 0% of each run, Pallas kernels for 75% -> 0%
where the time goes in v2:
time: 70.5 us; the launch traced here: 69.2 us
  Pallas kernels  66 us (94%)
  local copies, waits for them, and re-layouts  1.88 us (3%)
  between operations  1.3 us (2%)
    pallas_call x1, Pallas kernels, kernel_shards(): pl.pallas_call(functools.partial(fused_kernel, experts, capacity), out_sh...  66 us
    unnamed x1, local copies, waits for them, and re-layouts  1.88 us

profile of v2, /device:TPU:0, one launch (start us, length us, event | category | flops | bytes accessed | tf_op | source)
XLA Modules:
  0.0 69.2 jit_solution(18035707347257904436)
XLA Ops:
  1.3 66.0 %expert_layer.1 = bf16[1,128,2048]{2,1,0:T(8,128)(2,1)} custom-call(bf16[128,1024]{1,0:T(8,128)(2,1)} %tokens_ref.1, s32[2,128]{1,0:T(2,128)} %bitcast.8, f32[2,128]{1,0:T(2,128)} %bitcast.9, s32[1]{0:T(128)S(6)} %copy.13.length_ref, s32[1]{0:T(128)S(6)} %copy.14.page_ref, f32[1,1024]{1,0:T(1,128)} %bitcast.6, f32[1,1024]{1,0:T(1,128)} %bitcast.7, ...), custom_call_target="tpu_custom_call" | custom-call | flops 6442450944 | bytes 16777216 | tf_op jit(solution)/shard_map/expert_layer/pallas_call | solution.py:563
  67.3 1.9 %copy.15 = bf16[1,128,2048]{2,1,0:T(8,128)(2,1)} copy(bf16[1,128,2048]{2,1,0:T(8,128)(2,1)} %expert_layer.1) | data formatting | bytes 1048576

commit v3 on v2

--- a/solution.py
+++ b/solution.py
@@ -422,7 +422,6 @@
             back_send[step] = total
             back_copy(step).start()
 
-    order = unpaired + paired[1:]
     for step in unpaired:
         dispatch(step).start()
     for step in unpaired:
@@ -443,44 +442,53 @@
     for copy in swap_weights:
         copy.wait_recv()
     ffn_own(0)
-    for step in unpaired:
+    near, far = unpaired, paired[1:]
+    for step in near:
         dispatch(step).wait_recv()
         forward(step).start()
     got_other(0)
-    for step in unpaired:
+    for step in near:
         got_own(step)
-    previous = [0] + order[:-1]
-    for at, step in enumerate(order):
-        forward(previous[at]).wait_recv()
-        ffn_other(previous[at])
-        if at > 0:
-            finish(previous[at - 1])
-        if step in paired:
-            dispatch(step).wait_recv()
-            forward(step).start()
-            got_own(step)
+    for step in near:
         ffn_own(step)
-    for step in unpaired:
+        forward(step).wait_recv()
+        ffn_other(step)
+        if step == near[0]:
+            for distant in far:
+                dispatch(distant).wait_recv()
+                forward(distant).start()
+                got_own(distant)
+    for step in far:
+        ffn_own(step)
+    for step in near:
         got_other(step)
-    forward(order[-1]).wait_recv()
-    ffn_other(order[-1])
-    for step in paired[1:]:
+    for step in far:
+        forward(step).wait_recv()
+        ffn_other(step)
+    forward(0).wait_recv()
+    ffn_other(0)
+    finish(near[0])
+    got_part(1, 0)
+    for step in near[1:]:
+        finish(step)
+    for step in near:
+        got_part(0, step)
+    for step in far:
         got_other(step)
-    got_part(1, 0)
-    finish(previous[-1])
-    for step in unpaired:
+        finish(step)
+    for step in near:
+        got_part(1, step)
+    for step in far:
         got_part(0, step)
-    finish(order[-1])
-    for step in paired[1:]:
-        got_part(0, step)
-    for step in range(1, experts):
+    finish(0)
+    for step in far:
         got_part(1, step)
 
     logits = logits_t[...]
     gates = upright(jax.nn.sigmoid(logits[0:1] - logits[1:2]))
     gates_other = upright(jax.nn.sigmoid(logits[1:2] - logits[0:1]))
     residual = tok[...].astype(jnp.float32)
-    for step in [0] + order:
+    for step in near + [0] + far:
         if step > 0:
             back_copy(step).wait_recv()
         e = peer(step)

time: 70.5 us -> 68.5 us (0.972)
  Pallas kernels: 66 us -> 64 us
    pallas_call x1, Pallas kernels: 66 us -> 64 us  [kernel_shards(): pl.pallas_call(functools.partial(fused_kernel, experts, capacity), out_sh...]
where the time goes in v3:
time: 68.5 us; the launch traced here: 67.2 us
  Pallas kernels  64 us (93%)
  local copies, waits for them, and re-layouts  1.88 us (3%)
  between operations  1.3 us (2%)
    pallas_call x1, Pallas kernels, kernel_shards(): pl.pallas_call(functools.partial(fused_kernel, experts, capacity), out_sh...  64 us
    unnamed x1, local copies, waits for them, and re-layouts  1.88 us

profile of v3, /device:TPU:0, one launch (start us, length us, event | category | flops | bytes accessed | tf_op | source)
XLA Modules:
  0.0 67.2 jit_solution(11601527260529997427)
XLA Ops:
  1.3 64.0 %expert_layer.1 = bf16[1,128,2048]{2,1,0:T(8,128)(2,1)} custom-call(bf16[128,1024]{1,0:T(8,128)(2,1)} %tokens_ref.1, s32[2,128]{1,0:T(2,128)} %bitcast.8, f32[2,128]{1,0:T(2,128)} %bitcast.9, s32[1]{0:T(128)S(6)} %copy.13.length_ref, s32[1]{0:T(128)S(6)} %copy.14.page_ref, f32[1,1024]{1,0:T(1,128)} %bitcast.6, f32[1,1024]{1,0:T(1,128)} %bitcast.7, ...), custom_call_target="tpu_custom_call" | custom-call | flops 6442450944 | bytes 16777216 | tf_op jit(solution)/shard_map/expert_layer/pallas_call | solution.py:571
  65.3 1.9 %copy.15 = bf16[1,128,2048]{2,1,0:T(8,128)(2,1)} copy(bf16[1,128,2048]{2,1,0:T(8,128)(2,1)} %expert_layer.1) | data formatting | bytes 1048576

commit v4 on v3

--- a/solution.py
+++ b/solution.py
@@ -246,13 +246,6 @@
     ).astype(jnp.int32)
     slots = jnp.where(named, count, -1)
     slot_lane = lax.broadcasted_iota(jnp.int32, (rows, capacity), 1)
-    for e in range(experts):
-        chosen = (slots[:, e : e + 1] == slot_lane).astype(jnp.float32).astype(jnp.bfloat16)
-        pick[e] = chosen
-        sends[e] = lax.dot_general(
-            chosen, normed, (((0,), (0,)), ((), ())), preferred_element_type=jnp.float32
-        ).astype(jnp.bfloat16)
-
     pl.semaphore_wait(barrier, experts + 2)
 
     def remote(src, dst, send_sem, recv_sem, where):
@@ -422,19 +415,26 @@
             back_send[step] = total
             back_copy(step).start()
 
-    for step in unpaired:
-        dispatch(step).start()
-    for step in unpaired:
-        kv_z(step).start()
-    for step in paired[1:]:
-        dispatch(step).start()
-    for step in paired[1:]:
-        kv_z(step).start()
-    held[0, z] = sends[z]
-    forward(0).start()
-    kv_x(0).start()
     for copy in swap_weights:
         copy.start()
+    near, far = unpaired, paired[1:]
+    for step in near + [0] + far:
+        e = peer(step)
+        slot = jnp.sum(jnp.where(lane == e, slots, 0), axis=1, keepdims=True)
+        chosen = (slot == slot_lane).astype(jnp.float32).astype(jnp.bfloat16)
+        pick[e] = chosen
+        gathered = lax.dot_general(
+            chosen, normed, (((0,), (0,)), ((), ())), preferred_element_type=jnp.float32
+        ).astype(jnp.bfloat16)
+        if step == 0:
+            held[0, z] = gathered
+            forward(0).start()
+        else:
+            sends[e] = gathered
+            dispatch(step).start()
+    kv_x(0).start()
+    for step in near + far:
+        kv_z(step).start()
     load_block.start()
     kv_core(0, 0, 0).start()
     for copy in local_weights:
@@ -442,45 +442,41 @@
     for copy in swap_weights:
         copy.wait_recv()
     ffn_own(0)
-    near, far = unpaired, paired[1:]
     for step in near:
         dispatch(step).wait_recv()
         forward(step).start()
+        if step == near[0]:
+            forward(0).wait_recv()
+            ffn_other(0)
     got_other(0)
-    for step in near:
+    got_own(near[0])
+    ffn_own(near[0])
+    for step in far:
+        dispatch(step).wait_recv()
+        forward(step).start()
+    forward(near[0]).wait_recv()
+    ffn_other(near[0])
+    for step in near[1:] + far:
         got_own(step)
-    for step in near:
         ffn_own(step)
+    finish(0)
+    for step in far + near[1:]:
         forward(step).wait_recv()
         ffn_other(step)
-        if step == near[0]:
-            for distant in far:
-                dispatch(distant).wait_recv()
-                forward(distant).start()
-                got_own(distant)
-    for step in far:
-        ffn_own(step)
+    got_part(1, 0)
     for step in near:
         got_other(step)
-    for step in far:
-        forward(step).wait_recv()
-        ffn_other(step)
-    forward(0).wait_recv()
-    ffn_other(0)
     finish(near[0])
-    got_part(1, 0)
-    for step in near[1:]:
-        finish(step)
     for step in near:
         got_part(0, step)
     for step in far:
         got_other(step)
+    for step in far + near[1:]:
         finish(step)
     for step in near:
         got_part(1, step)
     for step in far:
         got_part(0, step)
-    finish(0)
     for step in far:
         got_part(1, step)
 
@@ -488,7 +484,7 @@
     gates = upright(jax.nn.sigmoid(logits[0:1] - logits[1:2]))
     gates_other = upright(jax.nn.sigmoid(logits[1:2] - logits[0:1]))
     residual = tok[...].astype(jnp.float32)
-    for step in near + [0] + far:
+    for step in [0] + near[:1] + far + near[1:]:
         if step > 0:
             back_copy(step).wait_recv()
         e = peer(step)

time: 68.5 us -> 68.7 us (level)
  no operation moved by 1% of the time
where the time goes in v4:
time: 68.7 us; the launch traced here: 67.4 us
  Pallas kernels  64.2 us (93%)
  local copies, waits for them, and re-layouts  1.88 us (3%)
  between operations  1.3 us (2%)
    pallas_call x1, Pallas kernels, kernel_shards(): pl.pallas_call(functools.partial(fused_kernel, experts, capacity), out_sh...  64.2 us
    unnamed x1, local copies, waits for them, and re-layouts  1.88 us

profile of v4, /device:TPU:0, one launch (start us, length us, event | category | flops | bytes accessed | tf_op | source)
XLA Modules:
  0.0 67.4 jit_solution(16411959771211434047)
XLA Ops:
  1.3 64.2 %expert_layer.1 = bf16[1,128,2048]{2,1,0:T(8,128)(2,1)} custom-call(bf16[128,1024]{1,0:T(8,128)(2,1)} %tokens_ref.1, s32[2,128]{1,0:T(2,128)} %bitcast.8, f32[2,128]{1,0:T(2,128)} %bitcast.9, s32[1]{0:T(128)S(6)} %copy.13.length_ref, s32[1]{0:T(128)S(6)} %copy.14.page_ref, f32[1,1024]{1,0:T(1,128)} %bitcast.6, f32[1,1024]{1,0:T(1,128)} %bitcast.7, ...), custom_call_target="tpu_custom_call" | custom-call | flops 6442450944 | bytes 16777216 | tf_op jit(solution)/shard_map/expert_layer/pallas_call | solution.py:567
  65.5 1.9 %copy.15 = bf16[1,128,2048]{2,1,0:T(8,128)(2,1)} copy(bf16[1,128,2048]{2,1,0:T(8,128)(2,1)} %expert_layer.1) | data formatting | bytes 1048576

commit v5 on v4

--- a/solution.py
+++ b/solution.py
@@ -349,21 +349,25 @@
             held.at[0, at], held.at[1, at], xs_sem.at[step], xr_sem.at[step], {"exp": across}
         )
 
-    def part_copy(step):
+    slab = capacity // 2
+
+    def part_copy(step, half):
+        lines = pl.ds(half * slab, slab)
         return remote(
-            part_send.at[step],
-            part_recv.at[step],
-            ps_sem.at[step],
-            pr_sem.at[step],
+            part_send.at[step, lines],
+            part_recv.at[step, lines],
+            ps_sem.at[half * experts + step],
+            pr_sem.at[half * experts + step],
             {"exp": across},
         )
 
-    def back_copy(step):
+    def back_copy(step, half):
+        lines = pl.ds(half * slab, slab)
         return remote(
-            back_send.at[step],
-            back.at[z],
-            bs_sem.at[step],
-            br_sem.at[step],
+            back_send.at[step, lines],
+            back.at[z, lines],
+            bs_sem.at[half * experts + step],
+            br_sem.at[half * experts + step],
             {"exp": 2 * peer(step) + side},
         )
 
@@ -404,16 +408,19 @@
             part_send[step, :, cols] = total.astype(jnp.bfloat16)
 
         ffn(1, peer(step), store)
-        part_copy(step).start()
+        for half in range(2):
+            part_copy(step, half).start()
 
     def finish(step):
-        part_copy(step).wait_recv()
-        total = (own_sum[step] + part_recv[step].astype(jnp.float32)).astype(jnp.bfloat16)
-        if step == 0:
-            back[z] = total
-        else:
-            back_send[step] = total
-            back_copy(step).start()
+        for half in range(2):
+            lines = pl.ds(half * slab, slab)
+            part_copy(step, half).wait_recv()
+            total = own_sum[step, lines] + part_recv[step, lines].astype(jnp.float32)
+            if step == 0:
+                back[z, lines] = total.astype(jnp.bfloat16)
+            else:
+                back_send[step, lines] = total.astype(jnp.bfloat16)
+                back_copy(step, half).start()
 
     for copy in swap_weights:
         copy.start()
@@ -486,7 +493,8 @@
     residual = tok[...].astype(jnp.float32)
     for step in [0] + near[:1] + far + near[1:]:
         if step > 0:
-            back_copy(step).wait_recv()
+            for half in range(2):
+                back_copy(step, half).wait_recv()
         e = peer(step)
         gate = jnp.where(first == e, gates, gates_other)
         residual += gate * jnp.dot(pick[e], back[e], preferred_element_type=jnp.float32)
@@ -522,10 +530,12 @@
         copy.wait_send()
     for step in range(experts):
         forward(step).wait_send()
-        part_copy(step).wait_send()
+        for half in range(2):
+            part_copy(step, half).wait_send()
+            if step > 0:
+                back_copy(step, half).wait_send()
         if step > 0:
             dispatch(step).wait_send()
-            back_copy(step).wait_send()
             kv_z(step).wait_send()
         if step in paired:
             kv_x(step).wait_send()
@@ -595,7 +605,8 @@
             dma((2,)),
             dma((2,)),
         ]
-        + [dma((experts,)) for _ in range(8)]
+        + [dma((experts,)) for _ in range(4)]
+        + [dma((2 * experts,)) for _ in range(4)]
         + [dma, dma, dma((6,)), dma]
         + [dma((experts,)) for _ in range(6)]
         + [dma((2 * experts,)) for _ in range(2)]
@@ -629,7 +640,7 @@
     tok_rows = args[0].shape[0]
     experts = lax.axis_size("exp") // 2
     capacity = 2 * max(1, (3 * tok_rows + experts - 1) // (2 * experts))
-    whole_tiles = capacity % 16 == 0 and args[9].shape[0] % 32 == 0
+    whole_tiles = capacity % 32 == 0 and args[9].shape[0] % 32 == 0
     if whole_tiles and experts == 4 and lax.axis_size("dec") == lax.axis_size("rep") == 2:
         return kernel_shards(capacity, *args)
     return shards(*args)

time: 68.7 us -> 67.8 us (0.987)
  Pallas kernels: 64.2 us -> 63.3 us
    pallas_call x1, Pallas kernels: 64.2 us -> 63.3 us  [kernel_shards(): pl.pallas_call(functools.partial(fused_kernel, experts, capacity), out_sh...]
where the time goes in v5:
time: 67.8 us; the launch traced here: 66.5 us
  Pallas kernels  63.3 us (93%)
  local copies, waits for them, and re-layouts  1.88 us (3%)
  between operations  1.3 us (2%)
    pallas_call x1, Pallas kernels, kernel_shards(): pl.pallas_call(functools.partial(fused_kernel, experts, capacity), out_sh...  63.3 us
    unnamed x1, local copies, waits for them, and re-layouts  1.88 us

profile of v5, /device:TPU:0, one launch (start us, length us, event | category | flops | bytes accessed | tf_op | source)
XLA Modules:
  0.0 66.5 jit_solution(10006095417713766711)
XLA Ops:
  1.3 63.3 %expert_layer.1 = bf16[1,128,2048]{2,1,0:T(8,128)(2,1)} custom-call(bf16[128,1024]{1,0:T(8,128)(2,1)} %tokens_ref.1, s32[2,128]{1,0:T(2,128)} %bitcast.8, f32[2,128]{1,0:T(2,128)} %bitcast.9, s32[1]{0:T(128)S(6)} %copy.13.length_ref, s32[1]{0:T(128)S(6)} %copy.14.page_ref, f32[1,1024]{1,0:T(1,128)} %bitcast.6, f32[1,1024]{1,0:T(1,128)} %bitcast.7, ...), custom_call_target="tpu_custom_call" | custom-call | flops 6442450944 | bytes 16777216 | tf_op jit(solution)/shard_map/expert_layer/pallas_call | solution.py:577
  64.6 1.9 %copy.15 = bf16[1,128,2048]{2,1,0:T(8,128)(2,1)} copy(bf16[1,128,2048]{2,1,0:T(8,128)(2,1)} %expert_layer.1) | data formatting | bytes 1048576

commit v6 on v5

--- a/solution.py
+++ b/solution.py
@@ -474,12 +474,13 @@
     for step in near:
         got_other(step)
     finish(near[0])
+    for step in far:
+        finish(step)
+        got_other(step)
+    for step in near[1:]:
+        finish(step)
     for step in near:
         got_part(0, step)
-    for step in far:
-        got_other(step)
-    for step in far + near[1:]:
-        finish(step)
     for step in near:
         got_part(1, step)
     for step in far:

time: 67.8 us -> 67.8 us (level)
  no operation moved by 1% of the time
where the time goes in v6:
time: 67.8 us; the launch traced here: 66.5 us
  Pallas kernels  63.3 us (93%)
  local copies, waits for them, and re-layouts  1.88 us (3%)
  between operations  1.3 us (2%)
    pallas_call x1, Pallas kernels, kernel_shards(): pl.pallas_call(functools.partial(fused_kernel, experts, capacity), out_sh...  63.3 us
    unnamed x1, local copies, waits for them, and re-layouts  1.88 us

profile of v6, /device:TPU:0, one launch (start us, length us, event | category | flops | bytes accessed | tf_op | source)
XLA Modules:
  0.0 66.5 jit_solution(547181974182020125)
XLA Ops:
  1.3 63.3 %expert_layer.1 = bf16[1,128,2048]{2,1,0:T(8,128)(2,1)} custom-call(bf16[128,1024]{1,0:T(8,128)(2,1)} %tokens_ref.1, s32[2,128]{1,0:T(2,128)} %bitcast.8, f32[2,128]{1,0:T(2,128)} %bitcast.9, s32[1]{0:T(128)S(6)} %copy.13.length_ref, s32[1]{0:T(128)S(6)} %copy.14.page_ref, f32[1,1024]{1,0:T(1,128)} %bitcast.6, f32[1,1024]{1,0:T(1,128)} %bitcast.7, ...), custom_call_target="tpu_custom_call" | custom-call | flops 6442450944 | bytes 16777216 | tf_op jit(solution)/shard_map/expert_layer/pallas_call | solution.py:578
  64.6 1.9 %copy.15 = bf16[1,128,2048]{2,1,0:T(8,128)(2,1)} copy(bf16[1,128,2048]{2,1,0:T(8,128)(2,1)} %expert_layer.1) | data formatting | bytes 1048576
